TPU v7x, 512 devices: a whole 4x8x8 slice. The times are simulated.
512 devices in a mesh: mem: 64 (over y_hi, z, core), gx: 8 (over y_lo, x).
Axes of the slice: x: 4, y: 8 (y_hi: 4, y_lo: 2; y = y_hi * 2 + y_lo), z: 8, core: 2. Of those that a mesh axis runs over, the one named last changes fastest.
Arguments:
- fields: float32 [64, 4, 128, 32, 128], P('mem', None, 'gx'), may hold values from -4 to 9
- precursor: float32 [12, 4096], P(None, 'mem'), may hold values from -5 to 5
- heights: int32 [128, 32], replicated, may hold values from 0 to 32
- param_index: int32 [64, 2], P('mem'), may hold values from 0 to 15
- drag_table: float32 [16], replicated, may hold values from 0.2 to 2
- rough_table: float32 [16], replicated, may hold values from 0.01 to 0.5
Outputs:
- advanced: float32 [64, 4, 128, 32, 128], P('mem', None, 'gx')
All inputs are finite; a program needn't handle non-finite values.
Results may differ from a plain program's by a relative error of at most 0.0003.
Values sent between devices are 32-bit elements; how exact they have to be, the bound alone decides.
No kernel may reach another device: no remote copies, remote signals or barrier semaphores. Data moves between devices by JAX's collectives and lax.ppermute only.
A program may use at most 64 MiB of HBM per device.

v0:
```python
import jax
import jax.numpy as jnp
from jax import lax
from jax.sharding import PartitionSpec as P

spacing = 2.0
time_step = 0.2
viscosity = 1.0
target_speed = 3.0
relax_time = 1.0
karman = 0.4
buoyancy = 0.0327


def extended_2(cells, sides, width):
    for axis, dim in sides:
        count = lax.axis_size(axis)
        ends = count - 1
        head = lax.slice_in_dim(cells, 0, width, axis=dim)
        tail = lax.slice_in_dim(cells, cells.shape[dim] - width, cells.shape[dim], axis=dim)
        cells = jnp.concatenate(
            [
                lax.ppermute(tail, axis, [(i, (i + 1) % count) for i in range(ends)]),
                cells,
                lax.ppermute(head, axis, [((i + 1) % count, i) for i in range(ends)]),
            ],
            axis=dim,
        )
    return cells


def tendency(extended, columns, drag_coef, surface_coef, forcing):
    length = extended.shape[1] - 6

    def shift_x(k):
        return extended[:, 3 + k : 3 + k + length]

    center = shift_x(0)

    def shift_y(k):
        return jnp.roll(center, -k, axis=2)

    speed_u = center[0:1]
    speed_v = center[1:2]
    speed_w = center[2:3]
    cen_x = (
        -shift_x(-3)
        + 9.0 * shift_x(-2)
        - 45.0 * shift_x(-1)
        + 45.0 * shift_x(1)
        - 9.0 * shift_x(2)
        + shift_x(3)
    ) / (60.0 * spacing)
    dis_x = (
        -shift_x(-3)
        + 6.0 * shift_x(-2)
        - 15.0 * shift_x(-1)
        + 20.0 * center
        - 15.0 * shift_x(1)
        + 6.0 * shift_x(2)
        - shift_x(3)
    ) / (60.0 * spacing)
    cen_y = (
        -shift_y(-3)
        + 9.0 * shift_y(-2)
        - 45.0 * shift_y(-1)
        + 45.0 * shift_y(1)
        - 9.0 * shift_y(2)
        + shift_y(3)
    ) / (60.0 * spacing)
    dis_y = (
        -shift_y(-3)
        + 6.0 * shift_y(-2)
        - 15.0 * shift_y(-1)
        + 20.0 * center
        - 15.0 * shift_y(1)
        + 6.0 * shift_y(2)
        - shift_y(3)
    ) / (60.0 * spacing)
    padded = jnp.pad(center, ((0, 0), (0, 0), (0, 0), (1, 1)))
    above = padded[..., 2:]
    below = padded[..., :-2]
    advection = (
        speed_u * cen_x
        + jnp.abs(speed_u) * dis_x
        + speed_v * cen_y
        + jnp.abs(speed_v) * dis_y
        + speed_w * (above - below) / (2.0 * spacing)
    )
    laplacian = (
        shift_x(1) + shift_x(-1) + shift_y(1) + shift_y(-1) + above + below - 6.0 * center
    ) / (spacing * spacing)
    level = lax.broadcasted_iota(jnp.int32, center.shape[1:], 2)
    inside = (level < columns[:, :, None]).astype(jnp.float32)
    lowest = (level == 0).astype(jnp.float32)
    speed = jnp.sqrt(speed_u[0] * speed_u[0] + speed_v[0] * speed_v[0] + speed_w[0] * speed_w[0])
    horizontal = jnp.array([1.0, 1.0, 0.0, 0.0], jnp.float32)[:, None, None, None]
    first_only = jnp.array([1.0, 0.0, 0.0, 0.0], jnp.float32)[:, None, None, None]
    result = -advection + viscosity * laplacian - drag_coef * inside * speed * center
    result = result - surface_coef * speed * lowest * horizontal * center / spacing
    result = result + forcing * first_only
    lifted = buoyancy * center[3]
    result = result.at[2].add(lifted)
    return result


def coefficients(indices, drag_table, rough_table):
    slots = jnp.arange(drag_table.shape[0], dtype=jnp.int32)
    drag_coef = jnp.sum(jnp.where(slots == indices[0], drag_table, 0.0))
    rough = jnp.sum(jnp.where(slots == indices[1], rough_table, 0.0))
    surface_coef = (karman / jnp.log(0.5 * spacing / rough)) ** 2
    return (drag_coef, surface_coef)


def local(fields, precursor, heights, param_index, drag_table, rough_table):
    state = fields[0]
    width = state.shape[1]
    span = state.shape[2]
    levels = state.shape[3]
    tiles = lax.axis_size("gx")
    tile = lax.axis_index("gx")
    gathered = lax.all_gather(precursor, "mem", axis=1, tiled=True)
    plane = gathered.reshape(4, 3, span, levels)
    drag_coef, surface_coef = coefficients(param_index[0], drag_table, rough_table)
    count = tiles * width * span * levels
    padded_heights = jnp.pad(heights, ((6, 6), (0, 0)), mode="edge")
    is_first = tile == 0
    is_last = tile == tiles - 1
    begin = tile * width + 6 - 0
    columns = lax.dynamic_slice_in_dim(padded_heights, begin, width + 2 * 0, 0)
    current = state
    for fraction in (1.0 / 3.0, 0.5):
        total = lax.psum(jnp.sum(current[0]), "gx")
        forcing = (target_speed - total / count) / relax_time
        extended = extended_2(current, (("gx", 1),), 3)
        left = extended[:, :3]
        left = jnp.where(is_first, plane, left)
        right = extended[:, 3 + width :]
        edge = jnp.broadcast_to(extended[:, 3 + width - 1 : 3 + width], right.shape)
        right = jnp.where(is_last, edge, right)
        extended = jnp.concatenate([left, extended[:, 3 : 3 + width], right], axis=1)
        current = state + fraction * time_step * tendency(
            extended, columns, drag_coef, surface_coef, forcing
        )
    return current[None]


def solution(mesh):
    in_specs = (P("mem", None, "gx", None, None), P(None, "mem"), P(), P("mem", None), P(), P())
    out_specs = P("mem", None, "gx", None, None)
    return jax.shard_map(local, mesh=mesh, in_specs=in_specs, out_specs=out_specs, check_vma=False)
```

profile of v0, /device:TPU:8, one launch (start us, length us, event | category | flops | bytes accessed | tf_op | source)
XLA Modules:
  0.0 189.8 jit_solution(9042107590689729199)
XLA Ops:
  0.0 1.9 %fusion.37 = (f32[4,3,32,128]{3,2,1,0:T(8,128)}, f32[4,3,32,128]{3,2,1,0:T(8,128)}) fusion(f32[4,16,32,128]{3,2,1,0:T(8,128)} %bitcast.61), kind=kLoop, calls=%fused_computation.115 | loop fusion | bytes 786432 | tf_op jit(solution)/shard_map/slice | solution.py:19
  1.9 4.5 %collective-permute-start.1 = (f32[4,3,32,128]{3,2,1,0:T(8,128)}, f32[4,3,32,128]{3,2,1,0:T(8,128)}, u32[]{:S(2)}, u32[]{:S(2)}) collective-permute-start(f32[4,3,32,128]{3,2,1,0:T(8,128)} %get-tuple-element.61), channel_id=1, source_target_pairs={{1,0},{2,1},{3,2},{4,3},{5,4},{6,5},{7,6},{9,8},{10,9},{11,10},{12... | collective-permute-start | bytes 589832 | tf_op jit(solution)/shard_map/ppermute | solution.py:25
  6.5 1.9 %collective-permute-start = (f32[4,3,32,128]{3,2,1,0:T(8,128)}, f32[4,3,32,128]{3,2,1,0:T(8,128)}, u32[]{:S(2)}, u32[]{:S(2)}) collective-permute-start(f32[4,3,32,128]{3,2,1,0:T(8,128)} %get-tuple-element.62), channel_id=1, source_target_pairs={{0,1},{1,2},{2,3},{3,4},{4,5},{5,6},{6,7},{8,9},{9,10},{10,11},{11... | collective-permute-start | bytes 589832 | tf_op jit(solution)/shard_map/ppermute | solution.py:23
  8.4 1.5 slice_bitcast_fusion.3
  9.9 1.7 fusion.42
  11.6 0.7 fusion.38
  12.3 0.8 fusion.40
  13.0 1.7 multiply_bitcast_fusion.9
  14.7 0.2 fusion.41
  15.0 1.5 fusion.43
  16.5 1.5 fusion.39
  18.0 0.6 fusion.44
  18.5 1.2 fusion.29
  20.5 0.2 slice_reduce_fusion.2
  20.7 0.1 reshape.188
  20.8 0.1 reshape.187
  20.8 0.1 fusion.27
  20.9 0.1 copy.17
  21.0 90.2 %all-gather = f32[64,64,12]{1,2,0:T(8,128)S(1)} all-gather(f32[1,64,12]{1,2,0:T(8,128)S(1)} %bitcast.74), channel_id=1, replica_groups=mesh['mem'=64,'gx'=8] {'mem'}, dimensions={0}, use_global_device_ids=true | all-gather | bytes 199680 | tf_op jit(solution)/shard_map/all_gather | solution.py:122
  111.2 0.1 copy.16
  111.4 0.9 reshape.190
  112.2 1.0 copy.19
  113.3 20.7 %psum.14 = f32[]{:T(128)} all-reduce(f32[]{:T(128)} %get-tuple-element.55), channel_id=1, replica_groups=mesh['mem'=64,'gx'=8] {'gx'}, use_global_device_ids=true, to_apply=%region_3.4 | all-reduce | flops 1 | bytes 8 | tf_op jit(solution)/shard_map/psum | solution.py:133
  133.9 1.3 fusion.28
  135.9 1.0 select_multiply_fusion
  136.9 0.7 broadcast_multiply_fusion.1
  137.5 1.0 broadcast_select_fusion.1
  138.5 1.0 broadcast_select_fusion.3
  139.5 5.2 %subtract_add_fusion.1 = f32[4,16,32,128]{3,2,1,0:T(8,128)S(1)} fusion(f32[4,16,32,128]{3,2,1,0:T(8,128)S(1)} %bitcast.69, f32[4,16,3,128]{3,2,1,0:T(4,128)} %get-tuple-element.68, f32[4,16,29,128]{3,2,1,0:T(8,128)S(1)} %get-tuple-element.70, f32[4,16,2,128]{3,2,1,0:T(2,128)} %get-tuple-element.64, f32[4,16,30,128]{3,2,1,0:T(8,128)} %get-tuple-element.66, ...), kind=kLoop, calls=%fused_computation.55 | loop fusion | flops 21233664 | bytes 10616864 | tf_op jit(solution)/shard_map/add | solution.py:101
  144.8 0.1 fusion.24
  144.8 0.2 multiply_add_fusion
  145.1 0.6 slice_bitcast_fusion.2
  145.7 0.7 fusion.35
  146.4 0.7 fusion.31
  147.0 0.7 fusion.33
  147.7 0.8 fusion.30
  148.5 2.9 %multiply_bitcast_fusion.5 = (f32[16,32,128]{2,1,0:T(8,128)}, f32[16,32,128]{2,1,0:T(8,128)}, f32[16,32,128]{2,1,0:T(8,128)}, f32[]{:T(128)}, f32[16,32,128]{2,1...) fusion(f32[4,16,32,128]{3,2,1,0:T(8,128)S(1)} %multiply_add_fusion, ...), kind=kLoop, calls=%fused_computation.76 | loop fusion | flops 1114111 | bytes 2624012 | tf_op jit(solution)/shard_map/mul | solution.py:84
  151.4 1.2 fusion.32
  152.6 1.5 fusion.34
  154.1 1.5 fusion.36
  155.6 1.9 %collective-permute-start.3 = (f32[4,3,32,128]{3,2,1,0:T(8,128)}, f32[4,3,32,128]{3,2,1,0:T(8,128)}, u32[]{:S(2)}, u32[]{:S(2)}) collective-permute-start(f32[4,3,32,128]{3,2,1,0:T(8,128)} %get-tuple-element.39), channel_id=1, source_target_pairs={{1,0},{2,1},{3,2},{4,3},{5,4},{6,5},{7,6},{9,8},{10,9},{11,10},{12... | collective-permute-start | bytes 589832 | tf_op jit(solution)/shard_map/ppermute | solution.py:25
  157.6 3.9 %collective-permute-start.2 = (f32[4,3,32,128]{3,2,1,0:T(8,128)}, f32[4,3,32,128]{3,2,1,0:T(8,128)}, u32[]{:S(2)}, u32[]{:S(2)}) collective-permute-start(f32[4,3,32,128]{3,2,1,0:T(8,128)} %get-tuple-element.40), channel_id=1, source_target_pairs={{0,1},{1,2},{2,3},{3,4},{4,5},{5,6},{6,7},{8,9},{9,10},{10,11},{11... | collective-permute-start | bytes 589832 | tf_op jit(solution)/shard_map/ppermute | solution.py:23
  161.5 18.6 %psum.15 = f32[]{:T(128)} all-reduce(f32[]{:T(128)} %get-tuple-element.34), channel_id=1, replica_groups=mesh['mem'=64,'gx'=8] {'gx'}, use_global_device_ids=true, to_apply=%region_5.6 | all-reduce | flops 1 | bytes 8 | tf_op jit(solution)/shard_map/psum | solution.py:133
  180.8 1.0 broadcast_select_fusion.2
  181.8 1.0 broadcast_select_fusion
  182.8 5.7 %subtract_add_fusion = f32[4,16,32,128]{3,2,1,0:T(8,128)S(1)} fusion(f32[4,16,32,128]{3,2,1,0:T(8,128)S(1)} %multiply_add_fusion, f32[4,16,3,128]{3,2,1,0:T(4,128)} %get-tuple-element.46, f32[4,16,29,128]{3,2,1,0:T(8,128)} %get-tuple-element.48, f32[4,16,2,128]{3,2,1,0:T(2,128)} %get-tuple-element.42, f32[4,16,30,128]{3,2,1,0:T(8,128)S(1)} %copy-done.3, ...), kind=kLoop, calls=%fused_computation.47 | loop fusion | flops 21233664 | bytes 10616864 | tf_op jit(solution)/shard_map/add | solution.py:101
  188.5 0.1 fusion.23
  188.6 1.2 add_bitcast_fusion
  (39 shorter events, 0.1 us)
Async XLA Ops:
  0.0 11.6 %copy-start = (f32[1,4,16,32,128]{4,3,2,1,0:T(8,128)S(1)}, f32[1,4,16,32,128]{4,3,2,1,0:T(8,128)}, u32[]{:S(2)}) copy-start(f32[1,4,16,32,128]{4,3,2,1,0:T(8,128)} %param.14) | copy-start | bytes 3145732
  1.9 135.6 %collective-permute-start.1 = (f32[4,3,32,128]{3,2,1,0:T(8,128)}, f32[4,3,32,128]{3,2,1,0:T(8,128)}, u32[]{:S(2)}, u32[]{:S(2)}) collective-permute-start(f32[4,3,32,128]{3,2,1,0:T(8,128)} %get-tuple-element.61), channel_id=1, source_target_pairs={{1,0},{2,1},{3,2},{4,3},{5,4},{6,5},{7,6},{9,8},{10,9},{11,10},{12... | collective-permute-start | bytes 589832 | tf_op jit(solution)/shard_map/ppermute | solution.py:25
  6.5 132.0 %collective-permute-start = (f32[4,3,32,128]{3,2,1,0:T(8,128)}, f32[4,3,32,128]{3,2,1,0:T(8,128)}, u32[]{:S(2)}, u32[]{:S(2)}) collective-permute-start(f32[4,3,32,128]{3,2,1,0:T(8,128)} %get-tuple-element.62), channel_id=1, source_target_pairs={{0,1},{1,2},{2,3},{3,4},{4,5},{5,6},{6,7},{8,9},{9,10},{10,11},{11... | collective-permute-start | bytes 589832 | tf_op jit(solution)/shard_map/ppermute | solution.py:23
  16.5 1.5 copy-start.12
  16.5 2.1 %copy-start.13 = (f32[16]{0:T(128)S(1)}, f32[16]{0:T(128)}, u32[]{:S(2)}) copy-start(f32[16]{0:T(128)} %param.19) | copy-start | bytes 196
  16.5 4.0 %copy-start.7 = (s32[128,32]{0,1:T(8,128)S(1)}, s32[128,32]{0,1:T(8,128)}, u32[]{:S(2)}) copy-start(s32[128,32]{0,1:T(8,128)} %param.16) | copy-start | bytes 49156
  16.5 4.5 %copy-start.10 = (f32[12,64]{1,0:T(8,128)S(1)}, f32[12,64]{1,0:T(8,128)}, u32[]{:S(2)}) copy-start(f32[12,64]{1,0:T(8,128)} %param.15) | copy-start | bytes 9220
  111.2 22.7 %copy-start.14 = (f32[16]{0:T(128)S(1)}, f32[16]{0:T(128)}, u32[]{:S(2)}) copy-start(f32[16]{0:T(128)} %param.18) | copy-start | bytes 196
  113.2 26.2 %copy-start.5 = (f32[4,16,3,128]{3,2,1,0:T(4,128)S(1)}, f32[4,16,3,128]{3,2,1,0:T(4,128)}, u32[]{:S(2)}) copy-start(f32[4,16,3,128]{3,2,1,0:T(4,128)} %get-tuple-element.67) | copy-start | bytes 294916
  113.2 26.2 %copy-start.6 = (f32[4,16,2,128]{3,2,1,0:T(2,128)S(1)}, f32[4,16,2,128]{3,2,1,0:T(2,128)}, u32[]{:S(2)}) copy-start(f32[4,16,2,128]{3,2,1,0:T(2,128)} %get-tuple-element.63) | copy-start | bytes 196612
  135.8 3.7 %copy-start.1 = (f32[4,16,31,128]{3,2,1,0:T(8,128)S(1)}, f32[4,16,31,128]{3,2,1,0:T(8,128)}, u32[]{:S(2)}) copy-start(f32[4,16,31,128]{3,2,1,0:T(8,128)} %get-tuple-element.73) | copy-start | bytes 3047428
  135.8 3.7 %copy-start.2 = (f32[4,16,31,128]{3,2,1,0:T(8,128)S(1)}, f32[4,16,31,128]{3,2,1,0:T(8,128)}, u32[]{:S(2)}) copy-start(f32[4,16,31,128]{3,2,1,0:T(8,128)} %get-tuple-element.74) | copy-start | bytes 3047428
  135.8 3.7 %copy-start.4 = (f32[16,32,128]{2,1,0:T(8,128)S(1)}, f32[16,32,128]{2,1,0:T(8,128)}, u32[]{:S(2)}) copy-start(f32[16,32,128]{2,1,0:T(8,128)} %get-tuple-element.53) | copy-start | bytes 786436
  135.8 3.7 %copy-start.8 = (f32[4,16,1,128]{3,2,1,0:T(1,128)S(1)}, f32[4,16,1,128]{3,2,1,0:T(1,128)}, u32[]{:S(2)}) copy-start(f32[4,16,1,128]{3,2,1,0:T(1,128)} %get-tuple-element.71) | copy-start | bytes 98308
  135.8 3.7 %copy-start.11 = (f32[4]{0:T(128)S(1)}, f32[4]{0:T(128)}, u32[]{:S(2)}) copy-start(f32[4]{0:T(128)} %constant.118.clone) | copy-start | bytes 52
  154.1 26.6 %copy-start.15 = (f32[4]{0:T(128)S(1)}, f32[4]{0:T(128)}, u32[]{:S(2)}) copy-start(f32[4]{0:T(128)} %constant.119.clone) | copy-start | bytes 52
  155.6 26.2 %collective-permute-start.3 = (f32[4,3,32,128]{3,2,1,0:T(8,128)}, f32[4,3,32,128]{3,2,1,0:T(8,128)}, u32[]{:S(2)}, u32[]{:S(2)}) collective-permute-start(f32[4,3,32,128]{3,2,1,0:T(8,128)} %get-tuple-element.39), channel_id=1, source_target_pairs={{1,0},{2,1},{3,2},{4,3},{5,4},{6,5},{7,6},{9,8},{10,9},{11,10},{12... | collective-permute-start | bytes 589832 | tf_op jit(solution)/shard_map/ppermute | solution.py:25
  157.6 23.2 %collective-permute-start.2 = (f32[4,3,32,128]{3,2,1,0:T(8,128)}, f32[4,3,32,128]{3,2,1,0:T(8,128)}, u32[]{:S(2)}, u32[]{:S(2)}) collective-permute-start(f32[4,3,32,128]{3,2,1,0:T(8,128)} %get-tuple-element.40), channel_id=1, source_target_pairs={{0,1},{1,2},{2,3},{3,4},{4,5},{5,6},{6,7},{8,9},{9,10},{10,11},{11... | collective-permute-start | bytes 589832 | tf_op jit(solution)/shard_map/ppermute | solution.py:23
  180.7 2.1 %copy-start.3 = (f32[4,16,30,128]{3,2,1,0:T(8,128)S(1)}, f32[4,16,30,128]{3,2,1,0:T(8,128)}, u32[]{:S(2)}) copy-start(f32[4,16,30,128]{3,2,1,0:T(8,128)} %get-tuple-element.44) | copy-start | bytes 2949124
  180.7 2.1 %copy-start.9 = (f32[4,16,1,128]{3,2,1,0:T(1,128)S(1)}, f32[4,16,1,128]{3,2,1,0:T(1,128)}, u32[]{:S(2)}) copy-start(f32[4,16,1,128]{3,2,1,0:T(1,128)} %get-tuple-element.49) | copy-start | bytes 98308
where the time goes:
time: 190 us
  blocking collectives  129 us (68%)
  other arithmetic  25.2 us (13%)
  local copies, waits for them, and re-layouts  20.4 us (11%)
  starting transfers between devices  12.3 us (6%)
  between operations  2.29 us (1%)
    all_gather x1, blocking collectives, local(): gathered = lax.all_gather(precursor, 'mem', axis=1, tiled=True)  90.2 us
    psum x2, blocking collectives, local(): total = lax.psum(jnp.sum(current[0]), 'gx')  39.3 us
    slice x12, local copies, waits for them, and re-layouts, shift_y(): return jnp.roll(center, -k, axis=2)  12.6 us
    add x2, other arithmetic, tendency(): result = result + forcing * first_only  10.9 us
    ppermute x2, starting transfers between devices, extended_2(): lax.ppermute(head, axis, [((i + 1) % count, i) for i in range(ends)])  6.45 us
    ppermute x2, starting transfers between devices, extended_2(): lax.ppermute(tail, axis, [(i, (i + 1) % count) for i in range(ends)])  5.84 us
    mul x2, other arithmetic, tendency(): speed_u * cen_x + jnp.abs(speed_u) * dis_x + speed_v * cen_y  4.57 us
  transfers between devices with their start and end apart: 4, of which 0 were waited for; matrix products, arithmetic and copies ran while one was open for 10% of the time, Pallas kernels for 0%

commit v1 on v0

v1 whole, which is shorter than its diff:
```python
import functools

import jax
import jax.numpy as jnp
from jax import lax
from jax.experimental import pallas as pl
from jax.experimental.pallas import tpu as pltpu
from jax.sharding import PartitionSpec as P

spacing = 2.0
time_step = 0.2
viscosity = 1.0
target_speed = 3.0
relax_time = 1.0
karman = 0.4
buoyancy = 0.0327

SUB = 8
FIRST = time_step / 3.0
SECOND = time_step / 2.0


def wrap_rows(ref, field, layer, span):
    ref[field, layer, pl.ds(SUB - 3, 3), :] = ref[field, layer, pl.ds(SUB + span - 3, 3), :]
    ref[field, layer, pl.ds(SUB + span, 3), :] = ref[field, layer, pl.ds(SUB, 3), :]


def direction(speed, scale, diffuse):
    slow = speed * scale
    size = jnp.abs(slow)
    near = 15.0 * size + diffuse
    wide = 45.0 * slow
    odd = 9.0 * slow
    even = 6.0 * size
    return (
        {
            1: near - wide,
            -1: near + wide,
            2: odd - even,
            -2: -(odd + even),
            3: size - slow,
            -3: size + slow,
        },
        20.0 * size,
    )


def stage_chunk(state, layer, chunk, step, drag, surface, levels):
    row = SUB + SUB * chunk

    def load(field, dx, dy):
        return state[field, layer + 3 + dx, pl.ds(row + dy, SUB), :]

    centre = [load(f, 0, 0) for f in range(4)]
    u, v, w = centre[:3]
    diffuse = step * viscosity / (spacing * spacing)
    scale = step / (60.0 * spacing)
    along_x, mid_x = direction(u, scale, diffuse)
    along_y, mid_y = direction(v, scale, diffuse)
    lane = lax.broadcasted_iota(jnp.int32, u.shape, 1)
    lift = w * (step / (2.0 * spacing))
    up = jnp.where(lane == levels - 1, 0.0, diffuse - lift)
    down = jnp.where(lane == 0, 0.0, diffuse + lift)
    speed = jnp.sqrt(u * u + v * v + w * w)
    middle = -(mid_x + mid_y + 6.0 * diffuse + speed * drag)
    middle_uv = middle - jnp.where(lane == 0, speed * surface, 0.0)
    out = []
    for f in range(4):
        s = centre[f]
        total = (middle_uv if f < 2 else middle) * s
        total = total + up * pltpu.roll(s, levels - 1, 1) + down * pltpu.roll(s, 1, 1)
        for k in (1, -1, 2, -2, 3, -3):
            total = total + along_x[k] * load(f, k, 0)
            total = total + along_y[k] * load(f, 0, k)
        if f == 2:
            total = total + (step * buoyancy) * centre[3]
        out.append(total)
    return out, centre


def forcing_of(parts, count):
    total = jnp.sum(parts[...])
    return (target_speed - total / count) / relax_time


def first_kernel(count, tiles, flags, coefs, fields, left, right, plane, drag, sums, section, partial, state):
    width, span, levels = fields.shape[1:]
    is_first = flags[0] == 0
    is_last = flags[0] == tiles - 1
    rows = pl.ds(SUB, span)

    for f in range(4):

        @pl.loop(0, width)
        def _(i):
            state[f, i + 6, rows, :] = fields[f, i]

        @pl.when(jnp.logical_not(is_first))
        def _():
            for i in range(6):
                state[f, i, rows, :] = left[f, i]

        @pl.when(is_first)
        def _():
            for i in range(3):
                state[f, i, rows, :] = plane[3 * f + i]
                state[f, i + 3, rows, :] = plane[3 * f + i]

        @pl.when(jnp.logical_not(is_last))
        def _():
            for i in range(6):
                state[f, width + 6 + i, rows, :] = right[f, i]

        @pl.when(is_last)
        def _():
            for i in range(6):
                state[f, width + 6 + i, rows, :] = fields[f, width - 1]

        @pl.loop(0, width + 12)
        def _(i):
            wrap_rows(state, f, i, span)

    added = FIRST * forcing_of(sums, count)
    surface = coefs[0]
    partial[...] = jnp.zeros_like(partial)

    @pl.loop(0, width + 6)
    def _(layer):
        own = jnp.logical_and(layer >= 3, layer < width + 3).astype(jnp.float32)
        for chunk in range(span // SUB):
            change, centre = stage_chunk(
                state, layer, chunk, FIRST, FIRST * drag[layer, pl.ds(SUB * chunk, SUB), :], FIRST * surface, levels
            )
            for f in range(4):
                value = centre[f] + change[f]
                if f == 0:
                    value = value + added
                    partial[...] += own * value
                section[f, layer, pl.ds(SUB + SUB * chunk, SUB), :] = value
        for f in range(4):
            wrap_rows(section, f, layer, span)

    @pl.when(is_first)
    def _():
        for f in range(4):
            for i in range(3):
                section[f, i] = state[f, i + 3]

    @pl.when(is_last)
    def _():
        for f in range(4):
            for i in range(3):
                section[f, width + 3 + i] = section[f, width + 2]


def second_kernel(coefs, fields, section, drag, out):
    width, span, levels = fields.shape[1:]
    surface = coefs[0]

    @pl.loop(0, width)
    def _(layer):
        for chunk in range(span // SUB):
            rows = pl.ds(SUB * chunk, SUB)
            change, _ = stage_chunk(
                section, layer, chunk, SECOND, SECOND * drag[layer + 3, rows, :], SECOND * surface, levels
            )
            for f in range(4):
                out[f, layer, rows, :] = fields[f, layer, rows, :] + change[f]


def last_kernel(count, sums, before, out):
    added = SECOND * forcing_of(sums, count)
    out[...] = before[...] + added


def coefficients(indices, drag_table, rough_table):
    slots = jnp.arange(drag_table.shape[0], dtype=jnp.int32)
    drag_coef = jnp.sum(jnp.where(slots == indices[0], drag_table, 0.0))
    rough = jnp.sum(jnp.where(slots == indices[1], rough_table, 0.0))
    surface_coef = (karman / jnp.log(0.5 * spacing / rough)) ** 2
    return (drag_coef, surface_coef)


def local(fields, precursor, heights, param_index, drag_table, rough_table):
    state = fields[0]
    width, span, levels = state.shape[1:]
    tiles = lax.axis_size("gx")
    members = lax.axis_size("mem")
    tile = lax.axis_index("gx")
    count = tiles * width * span * levels
    vmem = pl.BlockSpec(memory_space=pltpu.VMEM)
    smem = pl.BlockSpec(memory_space=pltpu.SMEM)
    f32 = jnp.float32

    ends = tiles - 1
    left = lax.ppermute(state[:, width - 6 :], "gx", [(i, i + 1) for i in range(ends)])
    right = lax.ppermute(state[:, :6], "gx", [(i + 1, i) for i in range(ends)])

    piece = precursor.size
    shards = jnp.broadcast_to(precursor.reshape(1, 1, piece), (members, 1, piece))
    gathered = lax.all_to_all(shards, "mem", 0, 0, tiled=True)
    plane = gathered.reshape(members, 12, piece // 12).transpose(1, 0, 2).reshape(12, span, levels)

    own = jnp.sum(state[0].reshape(-1, SUB, levels), axis=0)
    sums = lax.all_to_all(jnp.broadcast_to(own[None], (tiles, SUB, levels)), "gx", 0, 0, tiled=True)

    drag_coef, surface_coef = coefficients(param_index[0], drag_table, rough_table)
    padded_heights = jnp.pad(heights, ((3, 3), (0, 0)), mode="edge")
    columns = lax.dynamic_slice_in_dim(padded_heights, tile * width, width + 6, 0)
    level = lax.broadcasted_iota(jnp.int32, (width + 6, span, levels), 2)
    drag = jnp.where(level < columns[:, :, None], drag_coef, 0.0)
    coefs = (surface_coef / spacing).reshape(1)
    flags = tile.astype(jnp.int32).reshape(1)

    section, partial = pl.pallas_call(
        functools.partial(first_kernel, count, tiles),
        out_shape=(
            jax.ShapeDtypeStruct((4, width + 6, span + 2 * SUB, levels), f32),
            jax.ShapeDtypeStruct((SUB, levels), f32),
        ),
        in_specs=[smem, smem] + [vmem] * 6,
        out_specs=(vmem, vmem),
        scratch_shapes=[pltpu.VMEM((4, width + 12, span + 2 * SUB, levels), f32)],
        compiler_params=pltpu.CompilerParams(vmem_limit_bytes=24 * 2**20),
        cost_estimate=pl.CostEstimate(flops=20_000_000, bytes_accessed=6_000_000, transcendentals=0),
        name="first_stage",
    )(flags, coefs, state, left, right, plane, drag, sums)

    later = lax.all_to_all(jnp.broadcast_to(partial[None], (tiles, SUB, levels)), "gx", 0, 0, tiled=True)

    before = pl.pallas_call(
        second_kernel,
        out_shape=jax.ShapeDtypeStruct(state.shape, f32),
        in_specs=[smem] + [vmem] * 3,
        out_specs=vmem,
        compiler_params=pltpu.CompilerParams(vmem_limit_bytes=24 * 2**20),
        cost_estimate=pl.CostEstimate(flops=20_000_000, bytes_accessed=6_000_000, transcendentals=0),
        name="second_stage",
    )(coefs, state, section, drag)

    block = pl.BlockSpec((1, width, span, levels), lambda i: (0, 0, 0, 0))
    out = pl.pallas_call(
        functools.partial(last_kernel, count),
        grid=(1,),
        out_shape=jax.ShapeDtypeStruct(state.shape, f32),
        in_specs=[pl.BlockSpec((tiles, SUB, levels), lambda i: (0, 0, 0)), block],
        out_specs=block,
        input_output_aliases={1: 0},
        name="add_forcing",
    )(later, before)
    return out[None]


def solution(mesh):
    in_specs = (P("mem", None, "gx", None, None), P(None, "mem"), P(), P("mem", None), P(), P())
    out_specs = P("mem", None, "gx", None, None)
    return jax.shard_map(local, mesh=mesh, in_specs=in_specs, out_specs=out_specs, check_vma=False)
```

time: 190 us -> 69.4 us (0.37)
  the two profiles are of different devices: /device:TPU:8 before, /device:TPU:16 now
where the time goes in v1:
time: 69.4 us; the launch traced here: 68.9 us
  starting transfers between devices  31.8 us (46%)
  waiting for transfers between devices  12.5 us (18%)
  local copies, waits for them, and re-layouts  9.89 us (14%)
  Pallas kernels  9.88 us (14%)
  other arithmetic  3.96 us (6%)
  between operations  0.97 us (1%)
    all_to_all x1, starting transfers between devices, local(): gathered = lax.all_to_all(shards, 'mem', 0, 0, tiled=True)  16.5 us
    all_to_all x1, waiting for transfers between devices, local(): gathered = lax.all_to_all(shards, 'mem', 0, 0, tiled=True)  7.99 us
    all_to_all x1, starting transfers between devices, local(): lax.all_to_all(jnp.broadcast_to(own[None], (tiles, SUB, levels)), 'gx', 0...  7.27 us
    pallas_call x1, Pallas kernels, local(): pl.pallas_call(functools.partial(first_kernel, count, tiles), out_shape=(...  4.66 us
    unnamed x16, local copies, waits for them, and re-layouts  3.6 us
    ppermute x1, starting transfers between devices, local(): lax.ppermute(state[:, width - 6:], 'gx', [(i, i + 1) for i in range(ends)])  3.41 us
    pallas_call x1, Pallas kernels, local(): pl.pallas_call(second_kernel, out_shape=jax.ShapeDtypeStruct(state.shape,...  3.4 us
    all_to_all x1, starting transfers between devices, local(): lax.all_to_all(jnp.broadcast_to(partial[None], (tiles, SUB, levels)), 'gx...  3.32 us
  transfers between devices with their start and end apart: 5, of which 3 were waited for; matrix products, arithmetic and copies ran while one was open for 11% of the time, Pallas kernels for 5%

profile of v1, /device:TPU:16, one launch (start us, length us, event | category | flops | bytes accessed | tf_op | source)
XLA Modules:
  0.0 68.9 jit_solution(10492467770830577180)
XLA Ops:
  0.0 0.0 copy-start
  0.0 0.0 copy-start.3
  0.0 0.0 copy-start.5
  0.0 0.0 copy-start.6
  0.0 0.0 copy-start.7
  0.0 2.1 %fusion.5 = (f32[4,6,32,128]{3,2,1,0:T(8,128)}, f32[4,6,32,128]{3,2,1,0:T(8,128)}) fusion(f32[4,16,32,128]{3,2,1,0:T(8,128)} %bitcast.8), kind=kLoop, calls=%fused_computation.13 | loop fusion | bytes 1572864 | tf_op jit(solution)/shard_map/slice | solution.py:197
  2.2 3.4 %collective-permute-start = (f32[4,6,32,128]{3,2,1,0:T(8,128)}, f32[4,6,32,128]{3,2,1,0:T(8,128)S(1)}, u32[]{:S(2)}, u32[]{:S(2)}) collective-permute-start(f32[4,6,32,128]{3,2,1,0:T(8,128)} %get-tuple-element.12), channel_id=1, source_target_pairs={{0,1},{1,2},{2,3},{3,4},{4,5},{5,6},{6,7},{8,9},{9,10},{10,11},{11... | collective-permute-start | bytes 1179656 | tf_op jit(solution)/shard_map/ppermute | solution.py:196
  5.6 1.3 %collective-permute-start.1 = (f32[4,6,32,128]{3,2,1,0:T(8,128)}, f32[4,6,32,128]{3,2,1,0:T(8,128)S(1)}, u32[]{:S(2)}, u32[]{:S(2)}) collective-permute-start(f32[4,6,32,128]{3,2,1,0:T(8,128)} %get-tuple-element.11), channel_id=1, source_target_pairs={{1,0},{2,1},{3,2},{4,3},{5,4},{6,5},{7,6},{9,8},{10,9},{11,10},{12... | collective-permute-start | bytes 1179656 | tf_op jit(solution)/shard_map/ppermute | solution.py:197
  6.9 0.8 %broadcast_in_dim.41 = f32[768]{0:T(1024)S(1)} reshape(f32[12,64]{1,0:T(8,128)} %param.7) | data formatting | bytes 6144 | tf_op jit(solution)/shard_map/broadcast_in_dim | solution.py:200
  7.7 0.8 %broadcast_in_dim.42 = f32[64,1,768]{2,1,0:T(1,128)} broadcast(f32[768]{0:T(1024)S(1)} %broadcast_in_dim.41), dimensions={2} | broadcast | bytes 199680 | tf_op jit(solution)/shard_map/broadcast_in_dim | solution.py:200
  8.4 16.5 %all-to-all-start = ((f32[64,1,768]{2,1,0:T(1,128)}), f32[64,1,768]{2,1,0:T(1,128)S(1)}, u32[]{:S(2)}, u32[]{:S(2)}) async-start(f32[64,1,768]{2,1,0:T(1,128)} %broadcast_in_dim.42), calls=%async_computation | async-start | bytes 393216 | tf_op jit(solution)/shard_map/all_to_all | solution.py:201
  24.9 0.0 copy-done.3
  24.9 0.2 slice_reduce_fusion
  25.1 0.1 reshape.39
  25.2 0.1 reshape.40
  25.2 0.1 fusion.2
  25.3 0.0 copy-done.5
  25.4 0.6 fusion.6
  25.9 0.0 copy-done.6
  25.9 1.2 %fusion.4 = f32[]{:T(128)} fusion(f32[16]{0:T(128)S(1)} %copy-done.6, s32[]{:T(128)} %bitcast.5), kind=kLoop, calls=%fused_computation.12 | loop fusion | flops 47 | bytes 72 | tf_op jit(solution)/shard_map/reduce_sum | solution.py:178
  27.2 0.0 copy-done
  27.2 0.1 copy.12
  27.3 0.1 reduce_sum.29
  27.4 0.8 %fusion.drag = f32[22,32,128]{2,1,0:T(8,128)S(1)} fusion(f32[]{:T(128)} %fusion.4, s32[22,32]{1,0:T(8,128)S(1)} %copy.12), kind=kLoop, calls=%fused_computation.1 | loop fusion | flops 180224 | bytes 363268 | tf_op jit(solution)/shard_map/jit(_where)/select_n | solution.py:211
  28.2 8.0 %all-to-all-done = f32[64,1,768]{2,1,0:T(1,128)S(1)} async-done(((f32[64,1,768]{2,1,0:T(1,128)}), f32[64,1,768]{2,1,0:T(1,128)S(1)}, u32[]{:S(2)}, u32[]{:S(2)}) %all-to-all-start) | async-done | bytes 196640 | tf_op jit(solution)/shard_map/all_to_all | solution.py:201
  36.2 0.6 broadcast_in_dim.45
  36.8 7.3 %all-to-all-start.1 = ((f32[8,8,128]{2,1,0:T(8,128)}), f32[8,8,128]{2,1,0:T(8,128)S(1)}, u32[]{:S(2)}, u32[]{:S(2)}) async-start(f32[8,8,128]{2,1,0:T(8,128)} %broadcast_in_dim.45), calls=%async_computation.1 | async-start | bytes 65536 | tf_op jit(solution)/shard_map/all_to_all | solution.py:205
  44.0 0.0 copy-done.7
  44.1 1.3 %fusion.3 = f32[]{:T(128)} fusion(f32[16]{0:T(128)S(1)} %copy-done.7, s32[]{:T(128)} %bitcast.1), kind=kLoop, calls=%fused_computation.11 | loop fusion | flops 47 | bytes 72 | tf_op jit(solution)/shard_map/reduce_sum | solution.py:179
  46.2 0.5 reduce
  46.6 0.1 reshape.37
  46.8 0.1 copy.11
  46.9 0.1 reshape.38.plane
  47.0 3.3 %all-to-all-done.1.sums = f32[8,8,128]{2,1,0:T(8,128)S(1)} async-done(((f32[8,8,128]{2,1,0:T(8,128)}), f32[8,8,128]{2,1,0:T(8,128)S(1)}, u32[]{:S(2)}, u32[]{:S(2)}) %all-to-all-start.1) | async-done | bytes 32800 | tf_op jit(solution)/shard_map/all_to_all | solution.py:205
  50.3 0.0 collective-permute-done.left
  50.3 0.0 collective-permute-done.1.right
  50.3 4.7 %first_stage.1 = (f32[4,22,48,128]{3,2,1,0:T(8,128)S(1)}, f32[8,128]{1,0:T(8,128)S(1)}) custom-call(s32[1]{0:T(128)} %bitcast.flags, f32[1]{0:T(128)} %bitcast.2.coefs, f32[4,16,32,128]{3,2,1,0:T(8,128)S(1)} %bitcast.9, f32[4,6,32,128]{3,2,1,0:T(8,128)S(1)} %collective-permute-done.left, f32[4,6,32,128]{3,2,1,0:T(8,128)S(1)} %collective-permute-done.1.right, ...), custom_call_target="tpu_custom_call" | custom-call | flops 20000000 | bytes 6000000 | tf_op jit(solution)/shard_map/first_stage/pallas_call | solution.py:215
  55.0 0.0 copy-start.1
  55.0 1.4 %copy-done.1 = f32[4,22,48,128]{3,2,1,0:T(8,128)} copy-done((f32[4,22,48,128]{3,2,1,0:T(8,128)}, f32[4,22,48,128]{3,2,1,0:T(8,128)S(1)}, u32[]{:S(2)}) %copy-start.1) | copy-done | bytes 2162712
  56.4 0.6 broadcast_in_dim.46
  57.0 3.3 %all-to-all-start.2 = ((f32[8,8,128]{2,1,0:T(8,128)}), f32[8,8,128]{2,1,0:T(8,128)S(1)}, u32[]{:S(2)}, u32[]{:S(2)}) async-start(f32[8,8,128]{2,1,0:T(8,128)} %broadcast_in_dim.46), calls=%async_computation.2 | async-start | bytes 65536 | tf_op jit(solution)/shard_map/all_to_all | solution.py:229
  60.3 0.0 copy-start.2
  60.3 1.6 %copy-done.2 = f32[4,22,48,128]{3,2,1,0:T(8,128)S(1)} copy-done((f32[4,22,48,128]{3,2,1,0:T(8,128)S(1)}, f32[4,22,48,128]{3,2,1,0:T(8,128)}, u32[]{:S(2)}) %copy-start.2) | copy-done | bytes 2162712
  61.9 3.4 %second_stage.1.before = f32[4,16,32,128]{3,2,1,0:T(8,128)} custom-call(f32[1]{0:T(128)} %bitcast.2.coefs, f32[4,16,32,128]{3,2,1,0:T(8,128)S(1)} %bitcast.10, f32[4,22,48,128]{3,2,1,0:T(8,128)S(1)} %copy-done.2, f32[22,32,128]{2,1,0:T(8,128)S(1)} %fusion.drag), custom_call_target="tpu_custom_call" | custom-call | flops 20000000 | bytes 6000000 | tf_op jit(solution)/shard_map/second_stage/pallas_call | solution.py:231
  65.3 1.2 %all-to-all-done.2.sums = f32[8,8,128]{2,1,0:T(8,128)S(1)} async-done(((f32[8,8,128]{2,1,0:T(8,128)}), f32[8,8,128]{2,1,0:T(8,128)S(1)}, u32[]{:S(2)}, u32[]{:S(2)}) %all-to-all-start.2) | async-done | bytes 32800 | tf_op jit(solution)/shard_map/all_to_all | solution.py:229
  66.5 0.0 copy-start.4
  66.5 0.6 copy-done.4
  67.1 1.8 %add_forcing.1 = f32[4,16,32,128]{3,2,1,0:T(8,128)} custom-call(f32[8,8,128]{2,1,0:T(8,128)} %copy-done.4, f32[4,16,32,128]{3,2,1,0:T(8,128)} %second_stage.1.before), custom_call_target="tpu_custom_call", output_to_operand_aliasing={{}: (1, {})} | custom-call | tf_op jit(solution)/shard_map/add_forcing/pallas_call | solution.py:242
  (1 shorter events, 0.0 us)
Async XLA Ops:
  0.0 27.2 %copy-start = (f32[1,4,16,32,128]{4,3,2,1,0:T(8,128)S(1)}, f32[1,4,16,32,128]{4,3,2,1,0:T(8,128)}, u32[]{:S(2)}) copy-start(f32[1,4,16,32,128]{4,3,2,1,0:T(8,128)} %param.6) | copy-start | bytes 3145732
  0.0 24.9 %copy-start.3 = (s32[128,32]{0,1:T(8,128)S(1)}, s32[128,32]{0,1:T(8,128)}, u32[]{:S(2)}) copy-start(s32[128,32]{0,1:T(8,128)} %param.8) | copy-start | bytes 49156
  0.0 25.3 %copy-start.5 = (s32[1,2]{1,0:T(1,128)S(1)}, s32[1,2]{1,0:T(1,128)}, u32[]{:S(2)}) copy-start(s32[1,2]{1,0:T(1,128)} %param.9) | copy-start | bytes 28
  0.0 25.9 %copy-start.6 = (f32[16]{0:T(128)S(1)}, f32[16]{0:T(128)}, u32[]{:S(2)}) copy-start(f32[16]{0:T(128)} %param.10) | copy-start | bytes 196
  0.0 44.0 %copy-start.7 = (f32[16]{0:T(128)S(1)}, f32[16]{0:T(128)}, u32[]{:S(2)}) copy-start(f32[16]{0:T(128)} %param.11) | copy-start | bytes 196
  2.2 48.1 %collective-permute-start = (f32[4,6,32,128]{3,2,1,0:T(8,128)}, f32[4,6,32,128]{3,2,1,0:T(8,128)S(1)}, u32[]{:S(2)}, u32[]{:S(2)}) collective-permute-start(f32[4,6,32,128]{3,2,1,0:T(8,128)} %get-tuple-element.12), channel_id=1, source_target_pairs={{0,1},{1,2},{2,3},{3,4},{4,5},{5,6},{6,7},{8,9},{9,10},{10,11},{11... | collective-permute-start | bytes 1179656 | tf_op jit(solution)/shard_map/ppermute | solution.py:196
  5.6 44.7 %collective-permute-start.1 = (f32[4,6,32,128]{3,2,1,0:T(8,128)}, f32[4,6,32,128]{3,2,1,0:T(8,128)S(1)}, u32[]{:S(2)}, u32[]{:S(2)}) collective-permute-start(f32[4,6,32,128]{3,2,1,0:T(8,128)} %get-tuple-element.11), channel_id=1, source_target_pairs={{1,0},{2,1},{3,2},{4,3},{5,4},{6,5},{7,6},{9,8},{10,9},{11,10},{12... | collective-permute-start | bytes 1179656 | tf_op jit(solution)/shard_map/ppermute | solution.py:197
  8.4 27.7 %all-to-all-start = ((f32[64,1,768]{2,1,0:T(1,128)}), f32[64,1,768]{2,1,0:T(1,128)S(1)}, u32[]{:S(2)}, u32[]{:S(2)}) async-start(f32[64,1,768]{2,1,0:T(1,128)} %broadcast_in_dim.42), calls=%async_computation | async-start | bytes 393216 | tf_op jit(solution)/shard_map/all_to_all | solution.py:201
  36.8 13.5 %all-to-all-start.1 = ((f32[8,8,128]{2,1,0:T(8,128)}), f32[8,8,128]{2,1,0:T(8,128)S(1)}, u32[]{:S(2)}, u32[]{:S(2)}) async-start(f32[8,8,128]{2,1,0:T(8,128)} %broadcast_in_dim.45), calls=%async_computation.1 | async-start | bytes 65536 | tf_op jit(solution)/shard_map/all_to_all | solution.py:205
  55.0 1.4 %copy-start.1 = (f32[4,22,48,128]{3,2,1,0:T(8,128)}, f32[4,22,48,128]{3,2,1,0:T(8,128)S(1)}, u32[]{:S(2)}) copy-start(f32[4,22,48,128]{3,2,1,0:T(8,128)S(1)} %get-tuple-element.8.section) | copy-start | bytes 6488068
  57.0 9.5 %all-to-all-start.2 = ((f32[8,8,128]{2,1,0:T(8,128)}), f32[8,8,128]{2,1,0:T(8,128)S(1)}, u32[]{:S(2)}, u32[]{:S(2)}) async-start(f32[8,8,128]{2,1,0:T(8,128)} %broadcast_in_dim.46), calls=%async_computation.2 | async-start | bytes 65536 | tf_op jit(solution)/shard_map/all_to_all | solution.py:229
  60.3 1.6 %copy-start.2 = (f32[4,22,48,128]{3,2,1,0:T(8,128)S(1)}, f32[4,22,48,128]{3,2,1,0:T(8,128)}, u32[]{:S(2)}) copy-start(f32[4,22,48,128]{3,2,1,0:T(8,128)} %copy-done.1) | copy-start | bytes 6488068
  66.5 0.6 copy-start.4

commit v2 on v1

v2 whole, which is shorter than its diff:
```python
import functools

import jax
import jax.numpy as jnp
from jax import lax
from jax.experimental import pallas as pl
from jax.experimental.pallas import tpu as pltpu
from jax.sharding import PartitionSpec as P

spacing = 2.0
time_step = 0.2
viscosity = 1.0
target_speed = 3.0
relax_time = 1.0
karman = 0.4
buoyancy = 0.0327

SUB = 8
REACH = 3
HALO = 2 * REACH
FIRST = time_step / 3.0
SECOND = time_step / 2.0
SHARD_ROWS = 64

SECTION_AT = 8
EIGHTH_AT = 16


def wrap_rows(ref, field, layer, span):
    ref[field, layer, pl.ds(SUB - REACH, REACH), :] = ref[field, layer, pl.ds(SUB + span - REACH, REACH), :]
    ref[field, layer, pl.ds(SUB + span, REACH), :] = ref[field, layer, pl.ds(SUB, REACH), :]


def direction(speed, step):
    slow = speed * (step / (60.0 * spacing))
    size = jnp.abs(slow)
    near = 15.0 * size + step * viscosity / (spacing * spacing)
    wide = 45.0 * slow
    odd = 9.0 * slow
    even = 6.0 * size
    weights = {
        1: near - wide,
        -1: near + wide,
        2: odd - even,
        -2: -(odd + even),
        3: size - slow,
        -3: size + slow,
    }
    return weights, 20.0 * size


def stage_chunk(state, layer, chunk, step, drag, surface, levels):
    row = SUB + SUB * chunk

    def load(field, dx, dy):
        return state[field, layer + REACH + dx, pl.ds(row + dy, SUB), :]

    centre = [load(f, 0, 0) for f in range(4)]
    u, v, w = centre[:3]
    diffuse = step * viscosity / (spacing * spacing)
    along_x, mid_x = direction(u, step)
    along_y, mid_y = direction(v, step)
    lane = lax.broadcasted_iota(jnp.int32, u.shape, 1)
    lift = w * (step / (2.0 * spacing))
    up = jnp.where(lane == levels - 1, 0.0, diffuse - lift)
    down = jnp.where(lane == 0, 0.0, diffuse + lift)
    speed = step * jnp.sqrt(u * u + v * v + w * w)
    middle = -(mid_x + mid_y + 6.0 * diffuse + speed * drag)
    middle_uv = middle - jnp.where(lane == 0, speed * surface, 0.0)
    out = []
    for f in range(4):
        s = centre[f]
        total = (middle_uv if f < 2 else middle) * s
        total = total + up * pltpu.roll(s, levels - 1, 1) + down * pltpu.roll(s, 1, 1)
        for k in (1, -1, 2, -2, 3, -3):
            total = total + along_x[k] * load(f, k, 0)
            total = total + along_y[k] * load(f, 0, k)
        if f == 2:
            total = total + (step * buoyancy) * centre[3]
        out.append(total)
    return out, centre


def from_inlet(u, layer, planes):
    along, _ = direction(u, FIRST)
    total = None
    for p in range(layer, REACH):
        term = along[p - REACH - layer] * planes[p]
        total = term if total is None else total + term
    return total


def forcing_of(total, count):
    return (target_speed - jnp.sum(total) / count) / relax_time


def total_of(ref, at):
    total = ref[0, pl.ds(at, SUB), :]
    for g in range(1, ref.shape[0]):
        total = total + ref[g, pl.ds(at, SUB), :]
    return total


def edges_kernel(fields, head, tail, state, sems):
    width = fields.shape[1]
    copies = [
        pltpu.make_async_copy(fields, state, sems.at[2]),
        pltpu.make_async_copy(fields.at[:, pl.ds(0, HALO)], head, sems.at[0]),
        pltpu.make_async_copy(fields.at[:, pl.ds(width - HALO, HALO)], tail, sems.at[1]),
    ]
    for copy in copies:
        copy.start()
    for copy in copies:
        copy.wait()


def inner_kernel(
    place, index, drag_table, rough_table, heights, fields, section, drag, surface, partial, sums, state, picks, drags, roughs, tops, sems
):
    width, span, levels = fields.shape[1:]
    copies = [
        pltpu.make_async_copy(source, target, sems.at[k])
        for k, (source, target) in enumerate(
            ((index, picks), (drag_table, drags), (rough_table, roughs), (heights, tops))
        )
    ]
    for copy in copies:
        copy.start()

    for f in range(4):

        @pl.loop(0, width, unroll=4)
        def _(i):
            state[f, i, pl.ds(SUB, span), :] = fields[f, i]
            wrap_rows(state, f, i, span)

    for copy in copies:
        copy.wait()
    rough = jnp.full((SUB, levels), roughs[picks[0, 1]], jnp.float32)
    ratio = karman / jnp.log(0.5 * spacing / rough)
    surface[...] = ratio * ratio / spacing
    coef = drags[picks[0, 0]]
    columns = tops.shape[1]
    level = lax.broadcasted_iota(jnp.int32, (span, levels), 1)
    here = pltpu.roll(tops[...], lax.rem(columns - place[0] * width, columns), 1)
    is_first = place[0] == 0
    is_last = (place[0] + 1) * width == columns
    for layer in range(-REACH, width + REACH):
        column = here[:, layer % columns : layer % columns + 1]
        if layer < 0:
            column = jnp.where(is_first, here[:, 0:1], column)
        if layer >= width:
            column = jnp.where(is_last, here[:, width - 1 : width], column)
        drag[layer + REACH] = jnp.where(level < column, coef, 0.0)

    total = [jnp.zeros(sums.shape, jnp.float32) for _ in range(4)]
    for layer in range(width):
        for c in range(span // SUB):
            total[c % 4] = total[c % 4] + fields[0, layer, pl.ds(SUB * c, SUB), :]
    sums[...] = (total[0] + total[1]) + (total[2] + total[3])
    partial[...] = jnp.zeros_like(partial)

    @pl.loop(0, width - HALO)
    def _(layer):
        at = layer + HALO
        for chunk in range(span // SUB):
            rows = pl.ds(SUB * chunk, SUB)
            change, centre = stage_chunk(state, layer, chunk, FIRST, drag[at, rows, :], surface[...], levels)
            for f in range(4):
                value = centre[f] + change[f]
                if f == 0:
                    partial[...] += value
                section[f, at, pl.ds(SUB + SUB * chunk, SUB), :] = value
        for f in range(4):
            wrap_rows(section, f, at, span)


def outer_kernel(tiles, place, drag, surface, fields, left, right, before, inner, section, sums, low, high):
    width, span, levels = fields.shape[1:]
    is_last = place[0] == tiles - 1
    rows = pl.ds(SUB, span)
    full = section.shape[1]

    for f in range(4):

        @pl.loop(0, HALO, unroll=True)
        def _(i):
            low[f, i, rows, :] = left[f, i]
            low[f, HALO + i, rows, :] = fields[f, i]
            high[f, i, rows, :] = fields[f, width - HALO + i]
            high[f, HALO + i, rows, :] = jnp.where(is_last, fields[f, width - 1], right[f, i])
            for ref in (low, high):
                wrap_rows(ref, f, i, span)
                wrap_rows(ref, f, HALO + i, span)

    sums[...] = inner[...]

    for ref, first_at, own in ((low, 0, (REACH, HALO)), (high, full - HALO, (0, REACH))):

        @pl.loop(0, HALO)
        def _(layer):
            at = first_at + layer
            mine = jnp.logical_and(layer >= own[0], layer < own[1]).astype(jnp.float32)
            for chunk in range(span // SUB):
                lines = pl.ds(SUB * chunk, SUB)
                change, centre = stage_chunk(ref, layer, chunk, FIRST, drag[at, lines, :], surface[...], levels)
                for f in range(4):
                    value = centre[f] + change[f]
                    if f == 0:
                        sums[...] += mine * value
                    section[f, at, pl.ds(SUB + SUB * chunk, SUB), :] = value
            for f in range(4):
                wrap_rows(section, f, at, span)

    @pl.when(is_last)
    def _():
        for f in range(4):
            for i in range(REACH):
                section[f, full - REACH + i] = section[f, full - REACH - 1]


def regroup_kernel(shards, eighth):
    per = shards.shape[0] // 2
    count = eighth.shape[0] // per
    for y in range(per):
        low, high = (shards[2 * y + h, pl.ds(0, count), :] for h in (0, 1))
        eighth[pl.ds(y, count, stride=per), :] = low + pltpu.roll(high, eighth.shape[1] // 2, 1)


def pack_kernel(first, second, fields, eighth, message):
    tiles = message.shape[0]
    span = fields.shape[2]
    lead_at = EIGHTH_AT + eighth.shape[0]
    for d in range(tiles):
        message[d, pl.ds(0, SUB), :] = first[...]
        message[d, pl.ds(SECTION_AT, SUB), :] = second[...]
        message[d, pl.ds(EIGHTH_AT, eighth.shape[0]), :] = eighth[...]
        for i in range(REACH):
            message[d, pl.ds(lead_at + span * i, span), :] = fields[0, i]


def second_kernel(
    count, place, drag, surface, fields, before, received, out, section, planes, result, sems
):
    tiles = received.shape[0]
    width, span, levels = fields.shape[1:]
    per = span // tiles
    lead_at = received.shape[1] - REACH * span
    is_first = place[0] == 0

    def assemble(r):
        for g in range(tiles):
            planes[r, pl.ds(per * g, per), :] = received[g, pl.ds(EIGHTH_AT + per * r, per), :]

    for r in range(REACH):
        assemble(r)
    extra = total_of(received, SECTION_AT)
    for c in range(span // SUB):
        rows = pl.ds(SUB * c, SUB)
        for i in range(REACH):
            lead = received[0, pl.ds(lead_at + span * i + SUB * c, SUB), :]
            extra = extra + from_inlet(lead, i, [planes[p, rows, :] for p in range(REACH)])
    added = FIRST * forcing_of(total_of(received, 0), count)
    forcing = SECOND * (forcing_of(extra, count) - added / relax_time)

    @pl.loop(0, section.shape[1], unroll=2)
    def _(at):
        section[0, at] = before[0, at] + added

    @pl.when(is_first)
    def _():
        for r in range(REACH, planes.shape[0]):
            assemble(r)
        for f in range(4):
            for i in range(REACH):
                section[f, i, pl.ds(SUB, span), :] = planes[REACH * f + i]
                section[f, REACH + i, pl.ds(SUB, span), :] += from_inlet(
                    fields[0, i], i, [planes[REACH * f + p] for p in range(REACH)]
                )
            for i in range(HALO):
                wrap_rows(section, f, i, span)

    copies = []
    step = width // sems.shape[0]
    for k in range(sems.shape[0]):

        @pl.loop(step * k, step * (k + 1))
        def _(layer):
            for chunk in range(span // SUB):
                rows = pl.ds(SUB * chunk, SUB)
                change, _ = stage_chunk(
                    section, layer, chunk, SECOND, drag[layer + REACH, rows, :], surface[...], levels
                )
                for f in range(4):
                    value = fields[f, layer, rows, :] + change[f]
                    if f == 0:
                        value = value + forcing
                    result[f, layer, rows, :] = value

        layers = pl.ds(step * k, step)
        copies.append(pltpu.make_async_copy(result.at[:, layers], out.at[:, layers], sems.at[k]))
        copies[-1].start()
    for copy in copies:
        copy.wait()


def local(fields, precursor, heights, param_index, drag_table, rough_table):
    state = fields[0]
    width, span, levels = state.shape[1:]
    tiles = lax.axis_size("gx")
    members = lax.axis_size("mem")
    tile = lax.axis_index("gx").astype(jnp.int32).reshape(1)
    count = tiles * width * span * levels
    f32 = jnp.float32
    vmem = pl.BlockSpec(memory_space=pltpu.VMEM)
    smem = pl.BlockSpec(memory_space=pltpu.SMEM)
    whole = pl.BlockSpec(memory_space=pl.ANY)
    tall = span + 2 * SUB
    full = width + HALO
    shape = jax.ShapeDtypeStruct
    params = pltpu.CompilerParams(vmem_limit_bytes=8 * 2**20)
    tile_sum = shape((SUB, levels), f32)

    blocks = members // tiles
    deal = [
        ((tiles * g + j) * tiles + b, (tiles * b + j) * tiles + g)
        for b in range(blocks)
        for j in range(tiles)
        for g in range(tiles)
    ]
    groups = [[tiles * b + j for j in range(tiles)] for b in range(blocks)]
    half = jnp.pad(precursor, ((0, SHARD_ROWS - precursor.shape[0]), (0, levels - precursor.shape[1])))
    shards = lax.all_to_all(
        jnp.broadcast_to(half[None], (tiles,) + half.shape), "mem", 0, 0, tiled=True, axis_index_groups=groups
    )
    eighth = pl.pallas_call(
        regroup_kernel,
        out_shape=shape((precursor.shape[0] * span // tiles, levels), f32),
        in_specs=[vmem],
        out_specs=vmem,
        compiler_params=pltpu.CompilerParams(vmem_limit_bytes=2 * 2**20),
        name="regroup",
    )(shards)
    eighth = lax.ppermute(eighth, ("mem", "gx"), deal)

    hbm = functools.partial(pltpu.with_memory_space_constraint, memory_space=pltpu.HBM)
    head, tail, state = pl.pallas_call(
        edges_kernel,
        out_shape=(shape((4, HALO, span, levels), f32), shape((4, HALO, span, levels), f32), shape(state.shape, f32)),
        in_specs=[whole],
        out_specs=(whole, whole, vmem),
        scratch_shapes=[pltpu.SemaphoreType.DMA((3,))],
        compiler_params=pltpu.CompilerParams(vmem_limit_bytes=4 * 2**20),
        name="edges",
    )(hbm(state))
    ends = tiles - 1
    left = lax.ppermute(tail, "gx", [(i, i + 1) for i in range(ends)])
    right = lax.ppermute(head, "gx", [(i + 1, i) for i in range(ends)])

    before, drag, surface, inner_sum, sums = pl.pallas_call(
        inner_kernel,
        out_shape=(
            shape((4, full, tall, levels), f32),
            shape((full, span, levels), f32),
            tile_sum,
            tile_sum,
            tile_sum,
        ),
        in_specs=[smem] + [whole] * 4 + [vmem],
        out_specs=(vmem,) * 5,
        scratch_shapes=[
            pltpu.VMEM((4, width, tall, levels), f32),
            pltpu.SMEM(param_index.shape, jnp.int32),
            pltpu.SMEM(drag_table.shape, f32),
            pltpu.SMEM(rough_table.shape, f32),
            pltpu.VMEM((span, heights.shape[0]), jnp.int32),
            pltpu.SemaphoreType.DMA((4,)),
        ],
        compiler_params=params,
        cost_estimate=pl.CostEstimate(flops=10_000_000, bytes_accessed=4_000_000, transcendentals=0),
        name="inner",
    )(tile, hbm(param_index), hbm(drag_table), hbm(rough_table), hbm(heights.T), state)

    section, outer_sum = pl.pallas_call(
        functools.partial(outer_kernel, tiles),
        out_shape=(shape((4, full, tall, levels), f32), tile_sum),
        in_specs=[smem] + [vmem] * 7,
        out_specs=(vmem, vmem),
        scratch_shapes=[
            pltpu.VMEM((4, 2 * HALO, tall, levels), f32),
            pltpu.VMEM((4, 2 * HALO, tall, levels), f32),
        ],
        input_output_aliases={6: 0},
        compiler_params=params,
        cost_estimate=pl.CostEstimate(flops=12_000_000, bytes_accessed=4_000_000, transcendentals=0),
        name="outer",
    )(tile, drag, surface, state, left, right, before, inner_sum)

    message = pl.pallas_call(
        pack_kernel,
        out_shape=shape((tiles, EIGHTH_AT + eighth.shape[0] + REACH * span, levels), f32),
        in_specs=[vmem] * 4,
        out_specs=vmem,
        compiler_params=params,
        name="pack",
    )(sums, outer_sum, state, eighth)
    received = lax.all_to_all(message, "gx", 0, 0, tiled=True)

    out, _ = pl.pallas_call(
        functools.partial(second_kernel, count),
        out_shape=(shape(state.shape, f32), shape(section.shape, f32)),
        in_specs=[smem] + [vmem] * 5,
        out_specs=(whole, vmem),
        scratch_shapes=[
            pltpu.VMEM((precursor.shape[0], span, levels), f32),
            pltpu.VMEM(state.shape, f32),
            pltpu.SemaphoreType.DMA((4,)),
        ],
        input_output_aliases={4: 1},
        compiler_params=params,
        name="second",
    )(tile, drag, surface, state, section, received)
    return out[None]


def solution(mesh):
    in_specs = (P("mem", None, "gx", None, None), P(None, "mem"), P(), P("mem", None), P(), P())
    out_specs = P("mem", None, "gx", None, None)
    return jax.shard_map(local, mesh=mesh, in_specs=in_specs, out_specs=out_specs, check_vma=False)
```

time: 69.4 us -> 53.7 us (0.77)
  blocking collectives: 0 us -> 21.1 us
  starting transfers between devices: 31.8 us -> 16.7 us
  local copies, waits for them, and re-layouts: 9.89 us -> 1.42 us
  waiting for transfers between devices: 12.5 us -> 4.44 us
  other arithmetic: 3.96 us -> 0 us
  between operations: 0.97 us -> 0.08 us
    all_to_all x0 -> x1, blocking collectives: none -> 21.1 us  [local(): received = lax.all_to_all(message, 'gx', 0, 0, tiled=True)]
    all_to_all x3 -> x1, starting transfers between devices: 27.1 us -> 7.27 us  [local(): lax.all_to_all(jnp.broadcast_to(half[None], (tiles,) + half.shape), 'mem'...]
    all_to_all x3 -> x1, waiting for transfers between devices: 12.4 us -> 3.55 us  [local(): lax.all_to_all(jnp.broadcast_to(half[None], (tiles,) + half.shape), 'mem'...]
    ppermute x2 -> x3, starting transfers between devices: 4.7 us -> 9.41 us  [the longest x1 4.69 us: local(): eighth = lax.ppermute(eighth, ('mem', 'gx'), deal)]
    unnamed x16 -> x0, local copies, waits for them, and re-layouts: 3.6 us -> none
    slice x4 -> x0, local copies, waits for them, and re-layouts: 2.92 us -> none  [the longest x1 2.14 us: local(): right = lax.ppermute(state[:, :6], 'gx', [(i + 1, i) for i in range(ends)])]
    reduce_sum x3 -> x0, other arithmetic: 2.61 us -> none  [the longest x1 1.3 us: coefficients(): rough = jnp.sum(jnp.where(slots == indices[1], rough_table, 0.0))]
    broadcast_in_dim x4 -> x1, local copies, waits for them, and re-layouts: 2.78 us -> 0.72 us  [local(): jnp.broadcast_to(half[None], (tiles,) + half.shape)]
  transfers between devices with their start and end apart: 5 -> 4, of which waited for: 3 -> 2; matrix products, arithmetic and copies ran while one was open for 11% -> 0% of each run, Pallas kernels for 5% -> 12%
where the time goes in v2:
time: 53.7 us; the launch traced here: 53.3 us
  blocking collectives  21.1 us (39%)
  starting transfers between devices  16.7 us (31%)
  Pallas kernels  9.63 us (18%)
  waiting for transfers between devices  4.44 us (8%)
  local copies, waits for them, and re-layouts  1.42 us (3%)
    all_to_all x1, blocking collectives, local(): received = lax.all_to_all(message, 'gx', 0, 0, tiled=True)  21.1 us
    all_to_all x1, starting transfers between devices, local(): lax.all_to_all(jnp.broadcast_to(half[None], (tiles,) + half.shape), 'mem'...  7.27 us
    ppermute x1, starting transfers between devices, local(): eighth = lax.ppermute(eighth, ('mem', 'gx'), deal)  4.69 us
    all_to_all x1, waiting for transfers between devices, local(): lax.all_to_all(jnp.broadcast_to(half[None], (tiles,) + half.shape), 'mem'...  3.55 us
    pallas_call x1, Pallas kernels, local(): pl.pallas_call(functools.partial(second_kernel, count), out_shape=(shape(...  3.43 us
    ppermute x1, starting transfers between devices, local(): left = lax.ppermute(tail, 'gx', [(i, i + 1) for i in range(ends)])  3.42 us
    pallas_call x1, Pallas kernels, local(): pl.pallas_call(inner_kernel, out_shape=(shape((4, full, tall, levels), f3...  2.61 us
    pallas_call x1, Pallas kernels, local(): pl.pallas_call(functools.partial(outer_kernel, tiles), out_shape=(shape((...  2.02 us
  transfers between devices with their start and end apart: 4, of which 2 were waited for; matrix products, arithmetic and copies ran while one was open for 0% of the time, Pallas kernels for 12%

profile of v2, /device:TPU:16, one launch (start us, length us, event | category | flops | bytes accessed | tf_op | source)
XLA Modules:
  0.0 53.3 jit_solution(13022634546543243605)
XLA Ops:
  0.0 0.7 %pad.4 = f32[64,128]{1,0:T(8,128)S(1)} pad(f32[12,64]{1,0:T(8,128)} %param.7, f32[]{:T(128)} %constant.6.clone.1), padding=0_52x0_64 | pad | bytes 35844 | tf_op jit(solution)/shard_map/jit(_pad)/pad | solution.py:332
  0.7 0.7 %broadcast_in_dim.4 = f32[8,64,128]{2,1,0:T(8,128)} broadcast(f32[64,128]{1,0:T(8,128)S(1)} %pad.4), dimensions={1,2} | broadcast | bytes 294912 | tf_op jit(solution)/shard_map/broadcast_in_dim | solution.py:334
  1.4 7.3 %all-to-all-start = ((f32[8,64,128]{2,1,0:T(8,128)}), f32[8,64,128]{2,1,0:T(8,128)S(1)}, u32[]{:S(2)}, u32[]{:S(2)}) async-start(f32[8,64,128]{2,1,0:T(8,128)} %broadcast_in_dim.4), calls=%async_computation | async-start | bytes 524288 | tf_op jit(solution)/shard_map/all_to_all | solution.py:333
  8.7 1.5 %edges.1 = (f32[4,6,32,128]{3,2,1,0:T(8,128)S(1)}, f32[4,6,32,128]{3,2,1,0:T(8,128)S(1)}, f32[4,16,32,128]{3,2,1,0:T(8,128)S(1)}) custom-call(f32[4,16,32,128]{3,2,1,0:T(8,128)} %bitcast.4), custom_call_target="tpu_custom_call" | custom-call | tf_op jit(solution)/shard_map/edges/pallas_call | solution.py:347
  10.2 3.4 %collective-permute-start = (f32[4,6,32,128]{3,2,1,0:T(8,128)S(1)}, f32[4,6,32,128]{3,2,1,0:T(8,128)S(1)}, u32[]{:S(2)}, u32[]{:S(2)}) collective-permute-start(f32[4,6,32,128]{3,2,1,0:T(8,128)S(1)} %get-tuple-element.19), channel_id=1, source_target_pairs={{0,1},{1,2},{2,3},{3,4},{4,5},{5,6},{6,7},{8,9},{9,10},{10,11},{11... | collective-permute-start | bytes 1179656 | tf_op jit(solution)/shard_map/ppermute | solution.py:357
  13.6 1.3 %collective-permute-start.1 = (f32[4,6,32,128]{3,2,1,0:T(8,128)S(1)}, f32[4,6,32,128]{3,2,1,0:T(8,128)S(1)}, u32[]{:S(2)}, u32[]{:S(2)}) collective-permute-start(f32[4,6,32,128]{3,2,1,0:T(8,128)S(1)} %get-tuple-element.20), channel_id=1, source_target_pairs={{1,0},{2,1},{3,2},{4,3},{5,4},{6,5},{7,6},{9,8},{10,9},{11,10},{12... | collective-permute-start | bytes 1179656 | tf_op jit(solution)/shard_map/ppermute | solution.py:358
  14.9 3.6 %all-to-all-done.shards = f32[8,64,128]{2,1,0:T(8,128)S(1)} async-done(((f32[8,64,128]{2,1,0:T(8,128)}), f32[8,64,128]{2,1,0:T(8,128)S(1)}, u32[]{:S(2)}, u32[]{:S(2)}) %all-to-all-start) | async-done | bytes 262176 | tf_op jit(solution)/shard_map/all_to_all | solution.py:333
  18.4 0.1 regroup.1
  18.5 4.7 %collective-permute-start.2 = (f32[48,128]{1,0:T(8,128)S(1)}, f32[48,128]{1,0:T(8,128)S(1)}, u32[]{:S(2)}, u32[]{:S(2)}) collective-permute-start(f32[48,128]{1,0:T(8,128)S(1)} %regroup.1), channel_id=1, source_target_pairs={{0,0},{64,1},{128,2},{192,3},{256,4},{320,5},{384,6},{448,7},{8,8}... | collective-permute-start | bytes 73736 | tf_op jit(solution)/shard_map/ppermute | solution.py:344
  23.2 2.6 %inner.1 = (f32[4,22,48,128]{3,2,1,0:T(8,128)S(1)}, f32[22,32,128]{2,1,0:T(8,128)S(1)}, f32[8,128]{1,0:T(8,128)S(1)}, f32[8,128]{1,0:T(8,128)S(1)}, f32[8,128]{1,0:T(8,128)S(1)}) custom-call(s32[1]{0:T(128)} %bitcast.place, s32[1,2]{1,0:T(1,128)} %index.1, f32[16]{0:T(128)} %drag_table.1, f32[16]{0:T(128)} %rough_table.1, s32[32,128]{1,0:T(8,128)} %bitcast.5, ...), custom_call_target="tpu_custom_call" | custom-call | flops 10000000 | bytes 4000000 | tf_op jit(solution)/shard_map/inner/pallas_call | solution.py:360
  25.8 0.0 collective-permute-done.left
  25.8 0.9 %collective-permute-done.1.right = f32[4,6,32,128]{3,2,1,0:T(8,128)S(1)} collective-permute-done((f32[4,6,32,128]{3,2,1,0:T(8,128)S(1)}, f32[4,6,32,128]{3,2,1,0:T(8,128)S(1)}, u32[]{:S(2)}, u32[]{:S(2)}) %collective-permute-start.1) | collective-permute-done | bytes 393248 | tf_op jit(solution)/shard_map/ppermute | solution.py:358
  26.7 2.0 %outer.1 = (f32[4,22,48,128]{3,2,1,0:T(8,128)S(1)}, f32[8,128]{1,0:T(8,128)S(1)}) custom-call(s32[1]{0:T(128)} %bitcast.place, f32[22,32,128]{2,1,0:T(8,128)S(1)} %get-tuple-element.17.drag, f32[8,128]{1,0:T(8,128)S(1)} %get-tuple-element.18.surface, f32[4,16,32,128]{3,2,1,0:T(8,128)S(1)} %get-tuple-element.16.fields, ...), custom_call_target="tpu_custom_call", output_to_operand_aliasing={{0}: (6, {})} | custom-call | flops 12000000 | bytes 4000000 | tf_op jit(solution)/shard_map/outer/pallas_call | solution.py:384
  28.7 0.0 collective-permute-done.2.eighth
  28.8 21.1 %all_to_all.10.received = f32[8,160,128]{2,1,0:T(8,128)S(1)} all-to-all(f32[8,160,128]{2,1,0:T(8,128)S(1)} %pack.1), channel_id=1, replica_groups=mesh['mem'=64,'gx'=8] {'gx'}, dimensions={0} | all-to-all | bytes 1310720 | tf_op jit(solution)/shard_map/all_to_all | solution.py:407
  49.9 3.4 %second.1 = (f32[4,16,32,128]{3,2,1,0:T(8,128)}, f32[4,22,48,128]{3,2,1,0:T(8,128)S(1)}) custom-call(s32[1]{0:T(128)} %bitcast.place, f32[22,32,128]{2,1,0:T(8,128)S(1)} %get-tuple-element.17.drag, f32[8,128]{1,0:T(8,128)S(1)} %get-tuple-element.18.surface, f32[4,16,32,128]{3,2,1,0:T(8,128)S(1)} %get-tuple-element.16.fields, ...), custom_call_target="tpu_custom_call", output_to_operand_aliasing={{1}: (4, {})} | custom-call | tf_op jit(solution)/shard_map/second/pallas_call | solution.py:409
  (1 shorter events, 0.0 us)
Async XLA Ops:
  1.4 17.0 %all-to-all-start = ((f32[8,64,128]{2,1,0:T(8,128)}), f32[8,64,128]{2,1,0:T(8,128)S(1)}, u32[]{:S(2)}, u32[]{:S(2)}) async-start(f32[8,64,128]{2,1,0:T(8,128)} %broadcast_in_dim.4), calls=%async_computation | async-start | bytes 524288 | tf_op jit(solution)/shard_map/all_to_all | solution.py:333
  10.2 15.7 %collective-permute-start = (f32[4,6,32,128]{3,2,1,0:T(8,128)S(1)}, f32[4,6,32,128]{3,2,1,0:T(8,128)S(1)}, u32[]{:S(2)}, u32[]{:S(2)}) collective-permute-start(f32[4,6,32,128]{3,2,1,0:T(8,128)S(1)} %get-tuple-element.19), channel_id=1, source_target_pairs={{0,1},{1,2},{2,3},{3,4},{4,5},{5,6},{6,7},{8,9},{9,10},{10,11},{11... | collective-permute-start | bytes 1179656 | tf_op jit(solution)/shard_map/ppermute | solution.py:357
  13.6 13.1 %collective-permute-start.1 = (f32[4,6,32,128]{3,2,1,0:T(8,128)S(1)}, f32[4,6,32,128]{3,2,1,0:T(8,128)S(1)}, u32[]{:S(2)}, u32[]{:S(2)}) collective-permute-start(f32[4,6,32,128]{3,2,1,0:T(8,128)S(1)} %get-tuple-element.20), channel_id=1, source_target_pairs={{1,0},{2,1},{3,2},{4,3},{5,4},{6,5},{7,6},{9,8},{10,9},{11,10},{12... | collective-permute-start | bytes 1179656 | tf_op jit(solution)/shard_map/ppermute | solution.py:358
  18.5 10.2 %collective-permute-start.2 = (f32[48,128]{1,0:T(8,128)S(1)}, f32[48,128]{1,0:T(8,128)S(1)}, u32[]{:S(2)}, u32[]{:S(2)}) collective-permute-start(f32[48,128]{1,0:T(8,128)S(1)} %regroup.1), channel_id=1, source_target_pairs={{0,0},{64,1},{128,2},{192,3},{256,4},{320,5},{384,6},{448,7},{8,8}... | collective-permute-start | bytes 73736 | tf_op jit(solution)/shard_map/ppermute | solution.py:344

commit v3 on v2

--- a/solution.py
+++ b/solution.py
@@ -20,7 +20,7 @@
 HALO = 2 * REACH
 FIRST = time_step / 3.0
 SECOND = time_step / 2.0
-SHARD_ROWS = 64
+SHARD_ROWS = 56
 
 SECTION_AT = 8
 EIGHTH_AT = 16
@@ -101,16 +101,25 @@
     return total
 
 
-def edges_kernel(fields, head, tail, state, sems):
+def edges_kernel(fields, precursor, head, tail, state, message, shard, padded, sems):
     width = fields.shape[1]
+    rows, lanes = shard.shape
     copies = [
+        pltpu.make_async_copy(precursor, shard, sems.at[3]),
         pltpu.make_async_copy(fields, state, sems.at[2]),
         pltpu.make_async_copy(fields.at[:, pl.ds(0, HALO)], head, sems.at[0]),
         pltpu.make_async_copy(fields.at[:, pl.ds(width - HALO, HALO)], tail, sems.at[1]),
     ]
     for copy in copies:
         copy.start()
-    for copy in copies:
+    padded[...] = jnp.zeros_like(padded)
+    copies[0].wait()
+    padded[pl.ds(0, rows), pl.ds(0, lanes)] = shard[...]
+    for d in range(message.shape[0]):
+        copy = pltpu.make_async_copy(padded, message.at[d, pl.ds(0, padded.shape[0])], sems.at[4 + d])
+        copy.start()
+        copies.append(copy)
+    for copy in copies[1:]:
         copy.wait()
 
 
@@ -329,10 +338,26 @@
         for g in range(tiles)
     ]
     groups = [[tiles * b + j for j in range(tiles)] for b in range(blocks)]
-    half = jnp.pad(precursor, ((0, SHARD_ROWS - precursor.shape[0]), (0, levels - precursor.shape[1])))
-    shards = lax.all_to_all(
-        jnp.broadcast_to(half[None], (tiles,) + half.shape), "mem", 0, 0, tiled=True, axis_index_groups=groups
-    )
+    hbm = functools.partial(pltpu.with_memory_space_constraint, memory_space=pltpu.HBM)
+    head, tail, state, message = pl.pallas_call(
+        edges_kernel,
+        out_shape=(
+            shape((4, HALO, span, levels), f32),
+            shape((4, HALO, span, levels), f32),
+            shape(state.shape, f32),
+            shape((tiles, SHARD_ROWS, levels), f32),
+        ),
+        in_specs=[whole, whole],
+        out_specs=(vmem, vmem, vmem, whole),
+        scratch_shapes=[
+            pltpu.VMEM(precursor.shape, f32),
+            pltpu.VMEM((2 * SUB, levels), f32),
+            pltpu.SemaphoreType.DMA((4 + tiles,)),
+        ],
+        compiler_params=pltpu.CompilerParams(vmem_limit_bytes=4 * 2**20),
+        name="edges",
+    )(hbm(state), hbm(precursor))
+    shards = lax.all_to_all(message, "mem", 0, 0, tiled=True, axis_index_groups=groups)
     eighth = pl.pallas_call(
         regroup_kernel,
         out_shape=shape((precursor.shape[0] * span // tiles, levels), f32),
@@ -343,16 +368,6 @@
     )(shards)
     eighth = lax.ppermute(eighth, ("mem", "gx"), deal)
 
-    hbm = functools.partial(pltpu.with_memory_space_constraint, memory_space=pltpu.HBM)
-    head, tail, state = pl.pallas_call(
-        edges_kernel,
-        out_shape=(shape((4, HALO, span, levels), f32), shape((4, HALO, span, levels), f32), shape(state.shape, f32)),
-        in_specs=[whole],
-        out_specs=(whole, whole, vmem),
-        scratch_shapes=[pltpu.SemaphoreType.DMA((3,))],
-        compiler_params=pltpu.CompilerParams(vmem_limit_bytes=4 * 2**20),
-        name="edges",
-    )(hbm(state))
     ends = tiles - 1
     left = lax.ppermute(tail, "gx", [(i, i + 1) for i in range(ends)])
     right = lax.ppermute(head, "gx", [(i + 1, i) for i in range(ends)])

time: 53.7 us -> 53.2 us (level)
  local copies, waits for them, and re-layouts: 1.42 us -> 0 us
  blocking collectives: 21.1 us -> 21.9 us
    all_to_all x1, blocking collectives: 21.1 us -> 21.9 us  [local(): received = lax.all_to_all(message, 'gx', 0, 0, tiled=True)]
    all_to_all x1, waiting for transfers between devices: 3.55 us -> 4.33 us  [local(): lax.all_to_all(message, 'mem', 0, 0, tiled=True, axis_index_groups=groups)]
    ppermute x1, waiting for transfers between devices: 0.88 us -> 0.11 us  [local(): right = lax.ppermute(head, 'gx', [(i + 1, i) for i in range(ends)])]
    broadcast_in_dim x1 -> x0, local copies, waits for them, and re-layouts: 0.72 us -> none  [local(): jnp.broadcast_to(half[None], (tiles,) + half.shape)]
    pad x1 -> x0, local copies, waits for them, and re-layouts: 0.7 us -> none  [local(): jnp.pad(precursor, ((0, SHARD_ROWS - precursor.shape[0]), (0, levels - pr...]
  transfers between devices with their start and end apart: 4 -> 4, of which waited for: 2 -> 2; matrix products, arithmetic and copies ran while one was open for 0% -> 0% of each run, Pallas kernels for 12% -> 9%
where the time goes in v3:
time: 53.2 us; the launch traced here: 52.8 us
  blocking collectives  21.9 us (41%)
  starting transfers between devices  16.7 us (31%)
  Pallas kernels  9.74 us (18%)
  waiting for transfers between devices  4.44 us (8%)
    all_to_all x1, blocking collectives, local(): received = lax.all_to_all(message, 'gx', 0, 0, tiled=True)  21.9 us
    all_to_all x1, starting transfers between devices, local(): lax.all_to_all(message, 'mem', 0, 0, tiled=True, axis_index_groups=groups)  7.28 us
    ppermute x1, starting transfers between devices, local(): eighth = lax.ppermute(eighth, ('mem', 'gx'), deal)  4.7 us
    all_to_all x1, waiting for transfers between devices, local(): lax.all_to_all(message, 'mem', 0, 0, tiled=True, axis_index_groups=groups)  4.33 us
    pallas_call x1, Pallas kernels, local(): pl.pallas_call(functools.partial(second_kernel, count), out_shape=(shape(...  3.43 us
    ppermute x1, starting transfers between devices, local(): left = lax.ppermute(tail, 'gx', [(i, i + 1) for i in range(ends)])  3.41 us
    pallas_call x1, Pallas kernels, local(): pl.pallas_call(inner_kernel, out_shape=(shape((4, full, tall, levels), f3...  2.61 us
    pallas_call x1, Pallas kernels, local(): pl.pallas_call(functools.partial(outer_kernel, tiles), out_shape=(shape((...  2.02 us
  transfers between devices with their start and end apart: 4, of which 2 were waited for; matrix products, arithmetic and copies ran while one was open for 0% of the time, Pallas kernels for 9%

profile of v3, /device:TPU:16, one launch (start us, length us, event | category | flops | bytes accessed | tf_op | source)
XLA Modules:
  0.0 52.8 jit_solution(894269900406631485)
XLA Ops:
  0.0 1.6 %edges.1 = (f32[4,6,32,128]{3,2,1,0:T(8,128)S(1)}, f32[4,6,32,128]{3,2,1,0:T(8,128)S(1)}, f32[4,16,32,128]{3,2,1,0:T(8,128)S(1)}, f32[8,56,128]{2,1,0:T(8,128)}) custom-call(f32[4,16,32,128]{3,2,1,0:T(8,128)} %bitcast.4, f32[12,64]{1,0:T(8,128)} %precursor.1), custom_call_target="tpu_custom_call" | custom-call | tf_op jit(solution)/shard_map/edges/pallas_call | solution.py:342
  1.6 7.3 %all-to-all-start = ((f32[8,56,128]{2,1,0:T(8,128)}), f32[8,56,128]{2,1,0:T(8,128)S(1)}, u32[]{:S(2)}, u32[]{:S(2)}) async-start(f32[8,56,128]{2,1,0:T(8,128)} %get-tuple-element.27), calls=%async_computation | async-start | bytes 458752 | tf_op jit(solution)/shard_map/all_to_all | solution.py:360
  8.9 3.4 %collective-permute-start = (f32[4,6,32,128]{3,2,1,0:T(8,128)S(1)}, f32[4,6,32,128]{3,2,1,0:T(8,128)S(1)}, u32[]{:S(2)}, u32[]{:S(2)}) collective-permute-start(f32[4,6,32,128]{3,2,1,0:T(8,128)S(1)} %get-tuple-element.20), channel_id=1, source_target_pairs={{0,1},{1,2},{2,3},{3,4},{4,5},{5,6},{6,7},{8,9},{9,10},{10,11},{11... | collective-permute-start | bytes 1179656 | tf_op jit(solution)/shard_map/ppermute | solution.py:372
  12.3 1.3 %collective-permute-start.1 = (f32[4,6,32,128]{3,2,1,0:T(8,128)S(1)}, f32[4,6,32,128]{3,2,1,0:T(8,128)S(1)}, u32[]{:S(2)}, u32[]{:S(2)}) collective-permute-start(f32[4,6,32,128]{3,2,1,0:T(8,128)S(1)} %get-tuple-element.21), channel_id=1, source_target_pairs={{1,0},{2,1},{3,2},{4,3},{5,4},{6,5},{7,6},{9,8},{10,9},{11,10},{12... | collective-permute-start | bytes 1179656 | tf_op jit(solution)/shard_map/ppermute | solution.py:373
  13.6 4.3 %all-to-all-done.shards = f32[8,56,128]{2,1,0:T(8,128)S(1)} async-done(((f32[8,56,128]{2,1,0:T(8,128)}), f32[8,56,128]{2,1,0:T(8,128)S(1)}, u32[]{:S(2)}, u32[]{:S(2)}) %all-to-all-start) | async-done | bytes 229408 | tf_op jit(solution)/shard_map/all_to_all | solution.py:360
  17.9 0.1 regroup.1
  18.0 4.7 %collective-permute-start.2 = (f32[48,128]{1,0:T(8,128)S(1)}, f32[48,128]{1,0:T(8,128)S(1)}, u32[]{:S(2)}, u32[]{:S(2)}) collective-permute-start(f32[48,128]{1,0:T(8,128)S(1)} %regroup.1), channel_id=1, source_target_pairs={{0,0},{64,1},{128,2},{192,3},{256,4},{320,5},{384,6},{448,7},{8,8}... | collective-permute-start | bytes 73736 | tf_op jit(solution)/shard_map/ppermute | solution.py:369
  22.7 2.6 %inner.1 = (f32[4,22,48,128]{3,2,1,0:T(8,128)S(1)}, f32[22,32,128]{2,1,0:T(8,128)S(1)}, f32[8,128]{1,0:T(8,128)S(1)}, f32[8,128]{1,0:T(8,128)S(1)}, f32[8,128]{1,0:T(8,128)S(1)}) custom-call(s32[1]{0:T(128)} %bitcast.place, s32[1,2]{1,0:T(1,128)} %index.1, f32[16]{0:T(128)} %drag_table.1, f32[16]{0:T(128)} %rough_table.1, s32[32,128]{1,0:T(8,128)} %bitcast.5, ...), custom_call_target="tpu_custom_call" | custom-call | flops 10000000 | bytes 4000000 | tf_op jit(solution)/shard_map/inner/pallas_call | solution.py:375
  25.3 0.0 collective-permute-done.left
  25.3 0.1 collective-permute-done.1.right
  25.4 2.0 %outer.1 = (f32[4,22,48,128]{3,2,1,0:T(8,128)S(1)}, f32[8,128]{1,0:T(8,128)S(1)}) custom-call(s32[1]{0:T(128)} %bitcast.place, f32[22,32,128]{2,1,0:T(8,128)S(1)} %get-tuple-element.18.drag, f32[8,128]{1,0:T(8,128)S(1)} %get-tuple-element.19.surface, f32[4,16,32,128]{3,2,1,0:T(8,128)S(1)} %get-tuple-element.17.fields, ...), custom_call_target="tpu_custom_call", output_to_operand_aliasing={{0}: (6, {})} | custom-call | flops 12000000 | bytes 4000000 | tf_op jit(solution)/shard_map/outer/pallas_call | solution.py:399
  27.4 0.0 collective-permute-done.2.eighth
  27.5 21.9 %all_to_all.10.received = f32[8,160,128]{2,1,0:T(8,128)S(1)} all-to-all(f32[8,160,128]{2,1,0:T(8,128)S(1)} %pack.1), channel_id=1, replica_groups=mesh['mem'=64,'gx'=8] {'gx'}, dimensions={0} | all-to-all | bytes 1310720 | tf_op jit(solution)/shard_map/all_to_all | solution.py:422
  49.4 3.4 %second.1 = (f32[4,16,32,128]{3,2,1,0:T(8,128)}, f32[4,22,48,128]{3,2,1,0:T(8,128)S(1)}) custom-call(s32[1]{0:T(128)} %bitcast.place, f32[22,32,128]{2,1,0:T(8,128)S(1)} %get-tuple-element.18.drag, f32[8,128]{1,0:T(8,128)S(1)} %get-tuple-element.19.surface, f32[4,16,32,128]{3,2,1,0:T(8,128)S(1)} %get-tuple-element.17.fields, ...), custom_call_target="tpu_custom_call", output_to_operand_aliasing={{1}: (4, {})} | custom-call | tf_op jit(solution)/shard_map/second/pallas_call | solution.py:424
  (1 shorter events, 0.0 us)
Async XLA Ops:
  1.6 16.3 %all-to-all-start = ((f32[8,56,128]{2,1,0:T(8,128)}), f32[8,56,128]{2,1,0:T(8,128)S(1)}, u32[]{:S(2)}, u32[]{:S(2)}) async-start(f32[8,56,128]{2,1,0:T(8,128)} %get-tuple-element.27), calls=%async_computation | async-start | bytes 458752 | tf_op jit(solution)/shard_map/all_to_all | solution.py:360
  8.9 16.4 %collective-permute-start = (f32[4,6,32,128]{3,2,1,0:T(8,128)S(1)}, f32[4,6,32,128]{3,2,1,0:T(8,128)S(1)}, u32[]{:S(2)}, u32[]{:S(2)}) collective-permute-start(f32[4,6,32,128]{3,2,1,0:T(8,128)S(1)} %get-tuple-element.20), channel_id=1, source_target_pairs={{0,1},{1,2},{2,3},{3,4},{4,5},{5,6},{6,7},{8,9},{9,10},{10,11},{11... | collective-permute-start | bytes 1179656 | tf_op jit(solution)/shard_map/ppermute | solution.py:372
  12.3 13.1 %collective-permute-start.1 = (f32[4,6,32,128]{3,2,1,0:T(8,128)S(1)}, f32[4,6,32,128]{3,2,1,0:T(8,128)S(1)}, u32[]{:S(2)}, u32[]{:S(2)}) collective-permute-start(f32[4,6,32,128]{3,2,1,0:T(8,128)S(1)} %get-tuple-element.21), channel_id=1, source_target_pairs={{1,0},{2,1},{3,2},{4,3},{5,4},{6,5},{7,6},{9,8},{10,9},{11,10},{12... | collective-permute-start | bytes 1179656 | tf_op jit(solution)/shard_map/ppermute | solution.py:373
  18.0 9.5 %collective-permute-start.2 = (f32[48,128]{1,0:T(8,128)S(1)}, f32[48,128]{1,0:T(8,128)S(1)}, u32[]{:S(2)}, u32[]{:S(2)}) collective-permute-start(f32[48,128]{1,0:T(8,128)S(1)} %regroup.1), channel_id=1, source_target_pairs={{0,0},{64,1},{128,2},{192,3},{256,4},{320,5},{384,6},{448,7},{8,8}... | collective-permute-start | bytes 73736 | tf_op jit(solution)/shard_map/ppermute | solution.py:369
